TPU v7x, 512 devices: a whole 4x8x8 slice. The times are simulated.
512 devices in a mesh: wide: 64 (over x, y, core), narrow: 8 (over z).
Axes of the slice: x: 4, y: 8, z: 8, core: 2. Of those that a mesh axis runs over, the one named last changes fastest.
Arguments:
- edge_msg: bfloat16 [131072, 1024], P(('wide', 'narrow')), may hold values from -6 to 6
- basis: bfloat16 [131072, 512], P(('wide', 'narrow')), may hold values from -1.5 to 1.5
- atom_h: bfloat16 [4096, 512], P('narrow'), may hold values from -6 to 6
- edge_source: int32 [131072], P(('wide', 'narrow')), may hold values from 0 to 4095
- edge_target: int32 [131072], P(('wide', 'narrow')), may hold values from 0 to 4095, as said below
- send_rows: int32 [512, 2048], P(('wide', 'narrow')), may hold values from 0 to 255
- trip_slot: int32 [131072, 32], P(('wide', 'narrow')), may hold values from 0 to 2047, as said below
- w_down: bfloat16 [1024, 64], replicated, may hold values from -0.1875 to 0.1875
- w_bil: bfloat16 [1024, 64], replicated, may hold values from -0.1875 to 0.1875
- w_up: bfloat16 [64, 1024], replicated, may hold values from -0.75 to 0.75
- w_atom_in: bfloat16 [1024, 512], replicated, may hold values from -0.1875 to 0.1875
- atom_gain: float32 [512], replicated, may hold values from 0.5 to 1.5
- w_atom: bfloat16 [512, 512], replicated, may hold values from -0.25 to 0.25
- w_src: bfloat16 [512, 1024], replicated, may hold values from -0.25 to 0.25
- w_tgt: bfloat16 [512, 1024], replicated, may hold values from -0.25 to 0.25
Outputs:
- edge_out: bfloat16 [131072, 1024], P(('wide', 'narrow'))
- atom_out: bfloat16 [4096, 512], P('narrow')
Inputs may be any that keep to these rules, and one draw needn't show every extreme that they name: `edge_target`: the edges of block b target atoms of the narrow block b % 8, that is (b % 8) * 512 to (b % 8 + 1) * 512 - 1, never outside that range, and never falling (sorted) within a block. `trip_slot`: for each receiving block and each wide index p, the slots p * 32 + c that its triplets use form a prefix c < count of 1 to 32 entries; every block has some p with all 32 used.
All inputs are finite; a program needn't handle non-finite values.
Results may differ from a plain program's by a relative error of at most 0.0065.
Values may be sent and summed in bfloat16 or wider, within the bound.
A program may use at most 64 MiB of HBM per device.

v0:
```python
import jax
import jax.numpy as jnp
from jax import lax
from jax.sharding import PartitionSpec as P


def in_blocks(x, dim, peers):
    before, after = (x.shape[:dim], x.shape[dim + 1 :])
    return jnp.moveaxis(x.reshape(*before, peers, -1, *after), dim, 0)


def sent_and_summed(x, axis, dim):
    pieces = in_blocks(x, dim, lax.axis_size(axis))
    arrived = lax.all_to_all(pieces, axis, split_axis=0, concat_axis=0, tiled=True)
    return arrived.sum(axis=0)


def copy_for_each(x, axis):
    copies = jnp.broadcast_to(x, (lax.axis_size(axis), *x.shape))
    return lax.all_to_all(copies, axis, split_axis=0, concat_axis=0, tiled=True)


def laid_out(pieces, dim):
    pieces = jnp.moveaxis(pieces, 0, dim)
    shape = pieces.shape
    return pieces.reshape(*shape[:dim], shape[dim] * shape[dim + 1], *shape[dim + 2 :])


def collect(x, axis, dim):
    pieces = copy_for_each(x, axis)
    return laid_out(pieces, dim)


def silu(value):
    return value / (1.0 + jnp.exp(-value))


def atom_update(sums, base_rows, atom_gain, w_atom):
    scale = lax.rsqrt(jnp.mean(sums * sums, axis=-1, keepdims=True) + 1e-06)
    normed = (sums * scale * atom_gain).astype(jnp.bfloat16)
    grown = silu(jnp.dot(normed, w_atom, preferred_element_type=jnp.float32))
    return (base_rows.astype(jnp.float32) + grown).astype(jnp.bfloat16)


def per_device(
    edge_msg,
    basis,
    atom_h,
    edge_source,
    edge_target,
    send_rows,
    trip_slot,
    w_down,
    w_bil,
    w_up,
    w_atom_in,
    atom_gain,
    w_atom,
    w_src,
    w_tgt,
):
    edge_count = edge_msg.shape[0]
    width_trip = w_down.shape[1]
    basis_count = w_bil.shape[0] // width_trip
    triplets = trip_slot.shape[1]
    atom_count = atom_h.shape[0]
    down = silu(jnp.dot(edge_msg, w_down, preferred_element_type=jnp.float32)).astype(jnp.bfloat16)
    outgoing = down[send_rows[0]]
    slot_count = outgoing.shape[0]
    outgoing = outgoing.reshape(slot_count // 2, 2 * width_trip)
    received = lax.all_to_all(outgoing, "wide", split_axis=0, concat_axis=0, tiled=True)
    received = received.reshape(slot_count, width_trip)
    other = received[trip_slot]
    weights = basis.reshape(edge_count, triplets, basis_count)
    mixed = jnp.einsum("etk,etc->ekc", weights, other, preferred_element_type=jnp.float32)
    mixed = mixed.reshape(edge_count, basis_count * width_trip).astype(jnp.bfloat16)
    trip = silu(jnp.dot(mixed, w_bil, preferred_element_type=jnp.float32)).astype(jnp.bfloat16)
    edge_mid = (
        edge_msg.astype(jnp.float32) + jnp.dot(trip, w_up, preferred_element_type=jnp.float32)
    ).astype(jnp.bfloat16)
    message = jnp.dot(edge_mid, w_atom_in, preferred_element_type=jnp.float32).astype(jnp.bfloat16)
    first_atom = lax.axis_index("narrow") * atom_count
    local_target = edge_target - first_atom
    one_hot = (local_target[:, None] == jnp.arange(atom_count, dtype=jnp.int32)[None, :]).astype(
        jnp.bfloat16
    )
    partial_sums = lax.dot_general(
        one_hot, message, (((0,), (0,)), ((), ())), preferred_element_type=jnp.float32
    )
    shares = sent_and_summed(partial_sums, "wide", 0)
    share_rows = shares.shape[0]
    base_rows = lax.dynamic_slice_in_dim(atom_h, lax.axis_index("wide") * share_rows, share_rows, 0)
    updated = atom_update(shares, base_rows, atom_gain, w_atom)
    atom_out = collect(updated, "wide", 0)
    every_atom = lax.all_gather(atom_out, "narrow", axis=0, tiled=True)
    source_rows = every_atom[edge_source]
    target_rows = jnp.dot(one_hot, atom_out, preferred_element_type=jnp.float32).astype(
        jnp.bfloat16
    )
    update = jnp.dot(source_rows, w_src, preferred_element_type=jnp.float32) + jnp.dot(
        target_rows, w_tgt, preferred_element_type=jnp.float32
    )
    edge_out = (edge_mid.astype(jnp.float32) + silu(update)).astype(jnp.bfloat16)
    return (edge_out, atom_out)


def solution(mesh):
    placed = (
        P(("wide", "narrow"), None),
        P(("wide", "narrow"), None),
        P("narrow", None),
        P(("wide", "narrow")),
        P(("wide", "narrow")),
        P(("wide", "narrow"), None),
        P(("wide", "narrow"), None),
        P(),
        P(),
        P(),
        P(),
        P(),
        P(),
        P(),
        P(),
    )
    return jax.shard_map(
        per_device,
        mesh=mesh,
        in_specs=placed,
        out_specs=(P(("wide", "narrow"), None), P("narrow", None)),
        check_vma=False,
    )
```

profile of v0, /device:TPU:1, one launch (start us, length us, event | category | flops | bytes accessed | tf_op | source)
XLA Modules:
  0.0 210.7 jit_solution(11101356525887430000)
XLA Ops:
  7.2 0.0 copy-start
  7.2 0.8 compare_select_fusion.1
  8.0 1.4 divide_convert_fusion.1
  9.4 0.1 copy.24
  9.5 0.0 copy-start.6
  9.5 0.0 copy-start.4
  9.5 6.2 %gather_fusion = bf16[2048,64]{1,0:T(8,128)(2,1)S(1)} fusion(bf16[256,64]{1,0:T(8,128)(2,1)S(1)} %copy.24, s32[2048]{0:T(1024)S(1)} %broadcast_clamp_fusion.1), kind=kCustom, calls=%fused_computation | custom fusion | bytes 532480 | tf_op jit(solution)/shard_map/gather | solution.py:68
  15.7 0.0 copy-start.8
  15.7 1.0 all_to_all.12
  16.7 11.6 %all-to-all-start = ((bf16[64,16,128]{2,1,0:T(8,128)(2,1)}), bf16[64,16,128]{2,1,0:T(8,128)(2,1)S(1)}, u32[]{:S(2)}, u32[]{:S(2)}) async-start(bf16[64,16,128]{2,1,0:T(8,128)(2,1)} %all_to_all.12), calls=%async_computation | async-start | bytes 524288 | tf_op jit(solution)/shard_map/all_to_all | solution.py:71
  28.3 0.0 copy-done.6
  28.3 0.1 copy.25
  28.4 0.1 reshape.75
  28.5 0.0 copy-done.4
  28.5 0.1 copy.26
  28.7 1.0 copy.27
  29.7 0.0 copy-done.8
  29.8 10.5 %all-to-all-done = bf16[64,16,128]{2,1,0:T(8,128)(2,1)S(1)} async-done(((bf16[64,16,128]{2,1,0:T(8,128)(2,1)}), bf16[64,16,128]{2,1,0:T(8,128)(2,1)S(1)}, u32[]{:S(2)}, u32[]{:S(2)}) %all-to-all-start) | async-done | bytes 262176 | tf_op jit(solution)/shard_map/all_to_all | solution.py:71
  40.3 0.2 reshape.61
  40.5 29.2 %gather_fusion.1 = bf16[8192,64]{1,0:T(8,128)(2,1)} fusion(bf16[2048,64]{1,0:T(8,128)(2,1)S(1)} %reshape.61, s32[8192]{0:T(1024)S(1)} %broadcast_clamp_fusion), kind=kCustom, calls=%fused_computation.1 | custom fusion | bytes 2129920 | tf_op jit(solution)/shard_map/gather | solution.py:73
  69.8 0.0 copy-start.5
  69.8 2.3 %fusion = bf16[256,16,64]{2,1,0:T(8,128)(2,1)S(1)} fusion(bf16[256,32,16]{1,2,0:T(8,128)(2,1)S(1)} %copy.27, bf16[256,32,64]{2,1,0:T(8,128)(2,1)} %bitcast.25), kind=kOutput, calls=%fused_computation.5 | convolution fusion | flops 17039360 | bytes 1835008 | tf_op jit(solution)/shard_map/etk,etc->ekc/dot_general | solution.py:75
  72.1 0.8 copy.28
  72.9 0.0 copy-done.5
  72.9 1.8 fusion.1
  74.7 0.0 copy-done
  74.7 1.7 convolution_bitcast_fusion
  76.4 0.0 copy-start.3
  76.4 0.0 copy-start.7
  76.4 6.2 %all-to-all-start.1 = ((f32[64,8,512]{2,1,0:T(8,128)}), f32[64,8,512]{2,1,0:T(8,128)S(1)}, u32[]{:S(2)}, u32[]{:S(2)}) async-start(f32[64,8,512]{2,1,0:T(8,128)} %convolution_bitcast_fusion), calls=%async_computation.1 | async-start | bytes 2097152 | tf_op jit(solution)/shard_map/all_to_all | solution.py:14
  82.6 0.0 copy-start.9
  82.6 0.0 all-gather.2.cloned.1.call-start
  82.7 28.5 %all-to-all-done.1 = f32[64,8,512]{2,1,0:T(8,128)S(1)} async-done(((f32[64,8,512]{2,1,0:T(8,128)}), f32[64,8,512]{2,1,0:T(8,128)S(1)}, u32[]{:S(2)}, u32[]{:S(2)}) %all-to-all-start.1) | async-done | bytes 1048608 | tf_op jit(solution)/shard_map/all_to_all | solution.py:14
  111.2 0.1 reduce_sum.18
  111.3 0.1 multiply_reduce_fusion
  111.4 0.0 copy-done.3
  111.4 0.0 copy-done.7
  111.4 0.9 add_convert_fusion.1
  112.4 0.0 copy-start.2
  112.4 23.6 %all_to_all.19 = bf16[64,8,512]{2,1,0:T(8,128)(2,1)} all-to-all(bf16[64,8,512]{2,1,0:T(8,128)(2,1)S(1)} %broadcast_in_dim.7), channel_id=1, replica_groups=mesh['wide'=64,'narrow'=8] {'wide'}, dimensions={0} | all-to-all | bytes 1048576 | tf_op jit(solution)/shard_map/all_to_all | solution.py:20
  135.9 0.0 all-gather.2.cloned.1.call-update
  136.0 0.0 copy-done.9
  136.0 0.0 copy-start.1
  136.0 58.5 %all-gather.2.cloned.1.call-done = bf16[4096,512]{1,0:T(8,128)(2,1)} async-done(((bf16[512,512]{1,0:T(8,128)(2,1)}), bf16[4096,512]{1,0:T(8,128)(2,1)}) %all-gather.2.cloned.1.call-update) | async-done | bytes 4194320 | tf_op jit(solution)/shard_map/all_gather | solution.py:95
  194.5 3.9 %gather_fusion.2 = bf16[256,512]{1,0:T(8,128)(2,1)S(1)} fusion(bf16[4096,512]{1,0:T(8,128)(2,1)} %all-gather.2.cloned.1.call-done, s32[1024]{0:T(1024)S(1)} %pad_clamp_fusion), kind=kCustom, calls=%fused_computation.2 | custom fusion | bytes 525312 | tf_op jit(solution)/shard_map/gather | solution.py:96
  198.5 0.0 copy-done.2
  198.5 1.4 fusion.12
  199.9 0.0 copy-done.1
  199.9 3.2 %add_convert_fusion = bf16[256,1024]{1,0:T(8,128)(2,1)} fusion(f32[256,1024]{1,0:T(8,128)} %fusion.12, bf16[512,1024]{1,0:T(8,128)(2,1)} %param.29, bf16[512,512]{1,0:T(8,128)(2,1)S(1)} %bitcast.27, bf16[256,1024]{1,0:T(8,128)(2,1)S(1)} %fusion.1, s32[256]{0:T(256)S(1)} %broadcast_subtract_fusion), kind=kOutput, calls=%fused_computation.11 | convolution fusion | flops 404750336 | bytes 3671040 | tf_op jit(solution)/shard_map/dot_general | solution.py:100
  203.0 0.8 copy.30
  (8 shorter events, 0.1 us)
Async XLA Ops:
  7.2 67.6 %copy-start = (bf16[1024,512]{1,0:T(8,128)(2,1)S(1)}, bf16[1024,512]{1,0:T(8,128)(2,1)}, u32[]{:S(2)}) copy-start(bf16[1024,512]{1,0:T(8,128)(2,1)} %param.25) | copy-start | bytes 3145732
  9.5 18.8 %copy-start.6 = (s32[256,32]{0,1:T(8,128)S(1)}, s32[256,32]{0,1:T(8,128)}, u32[]{:S(2)}) copy-start(s32[256,32]{0,1:T(8,128)} %param.21) | copy-start | bytes 98308
  9.5 19.0 %copy-start.4 = (bf16[256,512]{1,0:T(8,128)(2,1)S(1)}, bf16[256,512]{1,0:T(8,128)(2,1)}, u32[]{:S(2)}) copy-start(bf16[256,512]{1,0:T(8,128)(2,1)} %param.16) | copy-start | bytes 786436
  15.7 14.0 %copy-start.8 = (s32[256]{0:T(256)S(1)}, s32[256]{0:T(256)}, u32[]{:S(2)}) copy-start(s32[256]{0:T(256)} %param.19) | copy-start | bytes 3076
  16.7 23.6 %all-to-all-start = ((bf16[64,16,128]{2,1,0:T(8,128)(2,1)}), bf16[64,16,128]{2,1,0:T(8,128)(2,1)S(1)}, u32[]{:S(2)}, u32[]{:S(2)}) async-start(bf16[64,16,128]{2,1,0:T(8,128)(2,1)} %all_to_all.12), calls=%async_computation | async-start | bytes 524288 | tf_op jit(solution)/shard_map/all_to_all | solution.py:71
  69.8 3.2 %copy-start.5 = (bf16[64,1024]{1,0:T(8,128)(2,1)S(1)}, bf16[64,1024]{1,0:T(8,128)(2,1)}, u32[]{:S(2)}) copy-start(bf16[64,1024]{1,0:T(8,128)(2,1)} %param.24) | copy-start | bytes 393220
  76.4 35.0 %copy-start.3 = (bf16[512,512]{1,0:T(8,128)(2,1)S(1)}, bf16[512,512]{1,0:T(8,128)(2,1)}, u32[]{:S(2)}) copy-start(bf16[512,512]{1,0:T(8,128)(2,1)} %param.27) | copy-start | bytes 1572868
  76.4 35.0 %copy-start.7 = (f32[512]{0:T(512)S(1)}, f32[512]{0:T(512)}, u32[]{:S(2)}) copy-start(f32[512]{0:T(512)} %param.26) | copy-start | bytes 6148
  76.4 34.7 %all-to-all-start.1 = ((f32[64,8,512]{2,1,0:T(8,128)}), f32[64,8,512]{2,1,0:T(8,128)S(1)}, u32[]{:S(2)}, u32[]{:S(2)}) async-start(f32[64,8,512]{2,1,0:T(8,128)} %convolution_bitcast_fusion), calls=%async_computation.1 | async-start | bytes 2097152 | tf_op jit(solution)/shard_map/all_to_all | solution.py:14
  82.6 53.4 %copy-start.9 = (s32[256]{0:T(256)S(1)}, s32[256]{0:T(256)}, u32[]{:S(2)}) copy-start(s32[256]{0:T(256)} %param.18) | copy-start | bytes 3076
  82.6 111.9 %all-gather.2.cloned.1.call-start = ((), (), s32[]{:S(2)}) async-start(), calls=%async_computation.3 | async-start | bytes 4718592 | tf_op jit(solution)/shard_map/all_gather | solution.py:95
  112.4 86.1 %copy-start.2 = (bf16[512,1024]{1,0:T(8,128)(2,1)S(1)}, bf16[512,1024]{1,0:T(8,128)(2,1)}, u32[]{:S(2)}) copy-start(bf16[512,1024]{1,0:T(8,128)(2,1)} %param.28) | copy-start | bytes 3145732
  136.0 63.9 %copy-start.1 = (bf16[64,8,512]{2,1,0:T(8,128)(2,1)S(1)}, bf16[64,8,512]{2,1,0:T(8,128)(2,1)}, u32[]{:S(2)}) copy-start(bf16[64,8,512]{2,1,0:T(8,128)(2,1)} %all_to_all.19) | copy-start | bytes 1572868
Sparse Core Ops, SparseCore 0:
  136.1 58.3 all-gather.1
where the time goes:
time: 211 us
  waiting for transfers between devices  97.5 us (46%)
  local copies, waits for them, and re-layouts  43.8 us (21%)
  blocking collectives  23.6 us (11%)
  starting transfers between devices  17.8 us (8%)
  between operations  14.3 us (7%)
  matrix products  12.6 us (6%)
    all_gather x1, waiting for transfers between devices, per_device(): every_atom = lax.all_gather(atom_out, 'narrow', axis=0, tiled=True)  58.5 us
    gather x1, local copies, waits for them, and re-layouts, per_device(): other = received[trip_slot]  29.2 us
    all_to_all x1, waiting for transfers between devices, sent_and_summed(): lax.all_to_all(pieces, axis, split_axis=0, concat_axis=0, tiled=True)  28.5 us
    all_to_all x1, blocking collectives, copy_for_each(): return lax.all_to_all(copies, axis, split_axis=0, concat_axis=0, tiled=True)  23.6 us
    all_to_all x1, starting transfers between devices, per_device(): lax.all_to_all(outgoing, 'wide', split_axis=0, concat_axis=0, tiled=True)  11.6 us
    all_to_all x1, waiting for transfers between devices, per_device(): lax.all_to_all(outgoing, 'wide', split_axis=0, concat_axis=0, tiled=True)  10.5 us
    gather x1, local copies, waits for them, and re-layouts, per_device(): outgoing = down[send_rows[0]]  6.18 us
    all_to_all x1, starting transfers between devices, sent_and_summed(): lax.all_to_all(pieces, axis, split_axis=0, concat_axis=0, tiled=True)  6.16 us
  transfers between devices with their start and end apart: 3, of which 3 were waited for; matrix products, arithmetic and copies ran while one was open for 1% of the time, Pallas kernels for 0%

commit v1 on v0

v1 whole, which is shorter than its diff:
```python
import jax
import jax.numpy as jnp
from jax import lax
from jax.experimental import pallas as pl
from jax.experimental.pallas import tpu as pltpu
from jax.sharding import PartitionSpec as P

MESH = pl.DeviceIdType.MESH
BF16, F32, I32 = jnp.bfloat16, jnp.float32, jnp.int32
NX, NY, NZ = 4, 8, 8
WIDE = NX * NY * 2
EDGES, WIDTH, TRIP, BASIS, TRIPLETS, SLOTS = 256, 1024, 64, 16, 32, 32
ATOMS, ATOM_WIDTH, HALF, TILE = 512, 512, 256, 128


def silu(value):
    return value / (1.0 + jnp.exp(-value))


def dot(a, b):
    return jnp.dot(a, b, preferred_element_type=F32)


def iota(shape, dim):
    return lax.broadcasted_iota(I32, shape, dim)


def ones_where(mask):
    return jnp.where(mask, 1.0, 0.0).astype(BF16)


def remote(src, dst, send_sem, recv_sem, device):
    return pltpu.make_async_remote_copy(
        src_ref=src, dst_ref=dst, send_sem=send_sem, recv_sem=recv_sem,
        device_id=device, device_id_type=MESH,
    )


def mix_kernel(
    msg_ref, basis_ref, slot_ref, rows_ref, target_ref, w_down_ref, w_bil_ref, w_up_ref, w_in_ref,
    mid_ref, part_ref,
    out_buf, in_buf, table, spread, bands, q_buf, g_buf, mixed, send_sem, recv_sem,
):
    me, row = lax.axis_index("wide"), lax.axis_index("narrow")
    barrier = pltpu.get_barrier_semaphore()

    def greet(i, carry):
        pl.semaphore_signal(barrier, inc=1, device_id=(lax.rem(me + i, WIDE), row), device_id_type=MESH)
        return carry

    lax.fori_loop(1, WIDE, greet, 0)

    down = silu(dot(msg_ref[...], w_down_ref[...])).T
    twice = jnp.concatenate([down, down], axis=0).astype(BF16)
    low_lane = iota((16, TILE), 1) < TRIP
    for j in range(8):
        hot = ones_where(iota((EDGES, 256), 0) == rows_ref[:, j * 256 : (j + 1) * 256])
        picked = dot(twice, hot).T
        for p in range(8):
            first, second = picked[p * 32 : p * 32 + 16], picked[p * 32 + 16 : p * 32 + 32]
            out_buf[j * 8 + p] = jnp.where(low_lane, first, second).astype(BF16)

    pl.semaphore_wait(barrier, WIDE - 1)

    def copy_to(i):
        peer = lax.rem(me + i, WIDE)
        return peer, remote(out_buf.at[peer], in_buf.at[me], send_sem.at[peer], recv_sem.at[me], (peer, row))

    def send(i, carry):
        copy_to(i)[1].start()
        return carry

    lax.fori_loop(1, WIDE, send, 0)
    in_buf[me] = out_buf[me]

    spread[...] = ones_where((iota((512, 256), 0) >> 4) == (iota((512, 256), 1) & 31))
    key = iota((8, 512), 1) & 15
    band = (iota((TILE, 256), 0) & 7) == (iota((TILE, 256), 1) >> 5)

    def build(i, carry):
        two = basis_ref[pl.ds(pl.multiple_of(i * 16, 16), 16), :].astype(F32)
        for h in range(2):
            x = two[h * 8 : h * 8 + 8]
            tall = jnp.concatenate([jnp.where(key == k, x, 0.0) for k in range(BASIS)], axis=0)
            block = jnp.where(band, dot(tall.astype(BF16), spread[...]), 0.0)
            bands[pl.ds(pl.multiple_of(i * 256 + h * TILE, TILE), TILE), :] = block.astype(BF16)
        return carry

    lax.fori_loop(0, EDGES // 16, build, 0)

    slots = slot_ref[...]
    spread2 = ones_where(iota((TRIPLETS, 256), 0) == (iota((TRIPLETS, 256), 1) & 31))
    band2 = (iota((EDGES, 256), 0) & 7) == (iota((EDGES, 256), 1) >> 5)

    def flat(values):
        wide = jnp.where(band2, dot(values.astype(F32).astype(BF16), spread2), 0.0)
        return wide.reshape(EDGES // 8, 8, 256).sum(axis=1)

    q_buf[...] = (flat((slots >> 5) & 31) * 16.0 + flat(slots & 15)).astype(I32)
    g_buf[...] = flat(((slots >> 10) << 1) | ((slots >> 4) & 1)).astype(I32)

    def arrived(i, carry):
        peer = lax.rem(me + i, WIDE)
        remote(out_buf.at[peer], in_buf.at[peer], send_sem.at[peer], recv_sem.at[peer], (peer, row)).wait_recv()
        return carry

    lax.fori_loop(1, WIDE, arrived, 0)

    received = in_buf[...].reshape(WIDE * 16, TILE).astype(F32)
    table[...] = jnp.concatenate([received[:512].T, received[512:].T], axis=0).astype(BF16)
    low_lane8 = iota((8, TILE), 1) < TRIP

    def mix(i, carry):
        q, g = q_buf[pl.ds(i, 1), :], g_buf[pl.ds(i, 1), :]
        hot = ones_where(iota((512, 256), 0) == q)
        four = dot(table[...], hot)
        other = jnp.where(
            g < 2,
            jnp.where(g == 0, four[0:64], four[64:128]),
            jnp.where(g == 2, four[128:192], four[192:256]),
        )
        other = jnp.concatenate([other, other], axis=0).astype(BF16)
        block = bands[pl.ds(pl.multiple_of(i * TILE, TILE), TILE), :]
        got = lax.dot_general(block, other, (((1,), (1,)), ((), ())), preferred_element_type=F32)
        for k in range(8):
            pair = jnp.where(low_lane8, got[k * 16 : k * 16 + 8], got[k * 16 + 8 : k * 16 + 16])
            mixed[pl.ds(pl.multiple_of(i * 8, 8), 8), k * TILE : (k + 1) * TILE] = pair
        return carry

    lax.fori_loop(0, EDGES // 8, mix, 0)

    trip = silu(dot(mixed[...].astype(BF16), w_bil_ref[...])).astype(BF16)
    mid = (msg_ref[...].astype(F32) + dot(trip, w_up_ref[...])).astype(BF16)
    mid_ref[...] = mid
    message = dot(mid, w_in_ref[...]).astype(BF16)
    hot = ones_where(iota((ATOMS, EDGES), 0) == target_ref[...] - row * ATOMS)
    part_ref[...] = dot(hot, message)

    def sent(i, carry):
        copy_to(i)[1].wait_send()
        return carry

    lax.fori_loop(1, WIDE, sent, 0)


def atom_kernel(
    part_ref, mid_ref, source_ref, target_ref, atom_ref, gain_ref, w_atom_ref, w_src_ref, w_tgt_ref,
    edge_out, atom_out,
    snd1, rcv1, snd2, rcv2, snd3, rcv3, snd4, rcv4, all_a, all_b, sib_a, sib_b, src_sib, pick_snd, pick_rcv, col,
    s1, r1, s2, r2, s3, r3, s4, r4, si, ri, sa1, ra1, sb1, rb1, sa2, ra2, sb2, rb2, sring, rring, so, ro, sp, rp,
):
    wide, z = lax.axis_index("wide"), lax.axis_index("narrow")
    x, y, c = wide // 16, (wide // 2) % NY, wide % 2
    other = 1 - c

    def at(px, py, pc, pz):
        return (px * 16 + py * 2 + pc, pz)

    sibling = at(x, y, other, z)
    xs = [(lax.rem(x + i, NX), i) for i in range(1, NX)]
    ys = [(lax.rem(y + i, NY), i) for i in range(1, NY)]
    zs = [(lax.rem(z + i, NZ), i) for i in range(1, NZ)]
    peers = (
        [sibling]
        + [at(p, y, c, z) for p, _ in xs]
        + [at(x, p, c, z) for p, _ in ys]
        + [at(x, y, c, p) for p, _ in zs]
    )
    barrier = pltpu.get_barrier_semaphore()
    for peer in peers:
        pl.semaphore_signal(barrier, inc=1, device_id=peer, device_id_type=MESH)

    mine, theirs = pl.ds(pl.multiple_of(c * HALF, HALF), HALF), pl.ds(pl.multiple_of(other * HALF, HALF), HALF)
    snd1[...] = part_ref[:, theirs].astype(BF16)
    pl.semaphore_wait(barrier, len(peers))

    waiting = []

    def start(copy):
        copy.start()
        waiting.append(copy)

    start(remote(snd1, rcv1, s1, r1, sibling))
    start(remote(source_ref, src_sib, si, ri, sibling))
    remote(snd1, rcv1, s1, r1, sibling).wait_recv()

    sums = part_ref[:, mine] + rcv1[...].astype(F32)
    snd2[...] = sums.astype(BF16).reshape(NX, NY * 16, HALF)
    for p, _ in xs:
        start(remote(snd2.at[p], rcv2.at[x], s2.at[p], r2.at[x], at(p, y, c, z)))
    my_x = pl.ds(pl.multiple_of(x * TILE, TILE), TILE)
    total = part_ref[my_x, mine] + rcv1[my_x, :].astype(F32)
    for p, _ in xs:
        remote(snd2.at[p], rcv2.at[p], s2.at[p], r2.at[p], at(p, y, c, z)).wait_recv()
        total = total + rcv2[p].astype(F32)
    snd3[...] = total.astype(BF16).reshape(NY, 16, HALF)
    for p, _ in ys:
        start(remote(snd3.at[p], rcv3.at[y], s3.at[p], r3.at[y], at(x, p, c, z)))
    share = snd3[y].astype(F32)
    for p, _ in ys:
        remote(snd3.at[p], rcv3.at[p], s3.at[p], r3.at[p], at(x, p, c, z)).wait_recv()
        share = share + rcv3[p].astype(F32)
    snd4[...] = share
    start(remote(snd4, rcv4, s4, r4, sibling))

    remote(source_ref, src_sib, si, ri, sibling).wait_recv()
    for i, ref in enumerate((source_ref, src_sib, target_ref)):
        for h in range(2):
            line = ref[:, h * TILE : (h + 1) * TILE].astype(F32)
            turned = jnp.broadcast_to(line, (TILE, TILE)).T
            col[i * 2 + h] = turned.astype(I32)

    remote(snd4, rcv4, s4, r4, sibling).wait_recv()
    theirs4 = rcv4[...]
    squares = jnp.sum(share * share, axis=-1, keepdims=True) + jnp.sum(theirs4 * theirs4, axis=-1, keepdims=True)
    scale = lax.rsqrt(squares * (1.0 / ATOM_WIDTH) + 1e-06)
    norm_mine = (share * scale * gain_ref[:, mine]).astype(BF16)
    norm_theirs = (theirs4 * scale * gain_ref[:, theirs]).astype(BF16)
    grown = silu(dot(norm_mine, w_atom_ref[mine, mine]) + dot(norm_theirs, w_atom_ref[theirs, mine]))
    first = pl.multiple_of(x * TILE + y * 16, 16)
    fresh = (atom_ref[pl.ds(first, 16), mine].astype(F32) + grown).astype(BF16)
    all_a[z, x, y] = fresh[:, :TILE]
    all_b[z, x, y] = fresh[:, TILE:]

    for p, _ in xs:
        start(remote(all_a.at[z, x, y], all_a.at[z, x, y], sa1.at[p], ra1.at[x], at(p, y, c, z)))
    for p, _ in zs:
        start(remote(all_b.at[z, x, y], all_b.at[z, x, y], sb1.at[p], rb1.at[z], at(x, y, c, p)))
    for p, _ in xs:
        block = all_a.at[z, p, y]
        remote(block, block, sa1.at[p], ra1.at[p], at(p, y, c, z)).wait_recv()
    for p, _ in ys:
        block = all_a.at[z, :, y]
        start(remote(block, block, sa2.at[p], ra2.at[y], at(x, p, c, z)))
    for p, _ in zs:
        block = all_b.at[p, x, y]
        remote(block, block, sb1.at[p], rb1.at[p], at(x, y, c, p)).wait_recv()
    for p, _ in xs:
        block = all_b.at[:, x, y]
        start(remote(block, block, sb2.at[p], rb2.at[x], at(p, y, c, z)))

    def ring_copy(axis, way, step, half, sending):
        n, pos = (NZ, z) if axis == 0 else (NY, y)
        hop = 1 if way == 0 else n - 1
        back = step - 1 if sending else step
        block = lax.rem(pos + (n - back if way == 0 else back), n)
        part = pl.ds(half * 2, 2)
        view = all_a.at[block, part] if axis == 0 else all_b.at[:, part, block]
        to = lax.rem(pos + hop, n)
        device = at(x, y, c, to) if axis == 0 else at(x, to, c, z)
        index = ((axis * 2 + way) * 4 + step - 1) * 2 + half
        return remote(view, view, sring.at[index], rring.at[index], device)

    for p, _ in xs:
        block = all_b.at[:, p, y]
        remote(block, block, sb2.at[p], rb2.at[p], at(p, y, c, z)).wait_recv()
    for half in range(2):
        for way in range(2):
            start(ring_copy(1, way, 1, half, True))
    for p, _ in ys:
        block = all_a.at[z, :, p]
        remote(block, block, sa2.at[p], ra2.at[p], at(x, p, c, z)).wait_recv()
    for half in range(2):
        for way in range(2):
            start(ring_copy(0, way, 1, half, True))
    own_a = remote(all_a.at[z], sib_a, so.at[0], ro.at[0], sibling)
    start(own_a)
    for step in range(1, 5):
        for half in range(2):
            for axis in (1, 0):
                for way in range(2):
                    if step == 4 and half != way:
                        continue
                    ring_copy(axis, way, step, half, False).wait_recv()
                    if step < 3 or (step == 3 and half == way):
                        start(ring_copy(axis, way, step + 1, half, True))
    own_b = remote(all_b.at[z], sib_b, so.at[1], ro.at[1], sibling)
    start(own_b)

    lanes = iota((EDGES, ATOMS), 1)

    def column(i):
        halves = [jnp.concatenate([col[i * 2 + h]] * (ATOMS // TILE), axis=1) for h in range(2)]
        return jnp.concatenate(halves, axis=0)

    def rows_of(first_ref, second_ref):
        a, b = first_ref[...].reshape(ATOMS, TILE), second_ref[...].reshape(ATOMS, TILE)
        return jnp.concatenate([a, b], axis=1)

    def picked(i):
        total = jnp.zeros((EDGES, HALF), F32)
        for block in range(NZ):
            hot = ones_where(column(i) - block * ATOMS == lanes)
            total = total + dot(hot, rows_of(all_a.at[block], all_b.at[block]))
        return total.astype(BF16)

    pick_snd[...] = picked(1)
    start(remote(pick_snd, pick_rcv, sp, rp, sibling))
    update = dot(picked(0), w_src_ref[mine, :])
    own_a.wait_recv()
    own_b.wait_recv()
    hot = ones_where(column(2) - z * ATOMS == lanes)
    ours = rows_of(all_a.at[z], all_b.at[z])
    sibs = rows_of(sib_a, sib_b)
    atom_out[:, mine] = ours
    atom_out[:, theirs] = sibs
    update += dot(dot(hot, ours).astype(BF16), w_tgt_ref[mine, :])
    update += dot(dot(hot, sibs).astype(BF16), w_tgt_ref[theirs, :])
    remote(pick_snd, pick_rcv, sp, rp, sibling).wait_recv()
    update += dot(pick_rcv[...], w_src_ref[theirs, :])
    edge_out[...] = (mid_ref[...].astype(F32) + silu(update)).astype(BF16)
    for copy in waiting:
        copy.wait_send()


def dma(*shape):
    return pltpu.SemaphoreType.DMA(shape)


def per_device(
    edge_msg, basis, atom_h, edge_source, edge_target, send_rows, trip_slot,
    w_down, w_bil, w_up, w_atom_in, atom_gain, w_atom, w_src, w_tgt,
):
    vmem = pl.BlockSpec(memory_space=pltpu.VMEM)
    source = edge_source.reshape(1, EDGES)
    target = edge_target.reshape(1, EDGES)
    mid, partial = pl.pallas_call(
        mix_kernel,
        out_shape=(
            jax.ShapeDtypeStruct((EDGES, WIDTH), BF16),
            jax.ShapeDtypeStruct((ATOMS, ATOM_WIDTH), F32),
        ),
        in_specs=[vmem] * 9,
        out_specs=(vmem, vmem),
        scratch_shapes=[
            pltpu.VMEM((WIDE, 16, TILE), BF16),
            pltpu.VMEM((WIDE, 16, TILE), BF16),
            pltpu.VMEM((256, 512), BF16),
            pltpu.VMEM((512, 256), BF16),
            pltpu.VMEM((EDGES * BASIS, 256), BF16),
            pltpu.VMEM((EDGES // 8, 256), I32),
            pltpu.VMEM((EDGES // 8, 256), I32),
            pltpu.VMEM((EDGES, BASIS * TRIP), F32),
            dma(WIDE),
            dma(WIDE),
        ],
        compiler_params=pltpu.CompilerParams(
            collective_id=0, has_side_effects=True, vmem_limit_bytes=40 * 1024 * 1024
        ),
        name="mix",
    )(edge_msg, basis, trip_slot, send_rows, target, w_down, w_bil, w_up, w_atom_in)

    def every():
        return pltpu.VMEM((NZ, NX, NY, 16, TILE), BF16)

    def one():
        return pltpu.VMEM((NX, NY, 16, TILE), BF16)

    edge_out, atom_out = pl.pallas_call(
        atom_kernel,
        out_shape=(
            jax.ShapeDtypeStruct((EDGES, WIDTH), BF16),
            jax.ShapeDtypeStruct((ATOMS, ATOM_WIDTH), BF16),
        ),
        in_specs=[vmem] * 9,
        out_specs=(vmem, vmem),
        scratch_shapes=[
            pltpu.VMEM((ATOMS, HALF), BF16), pltpu.VMEM((ATOMS, HALF), BF16),
            pltpu.VMEM((NX, NY * 16, HALF), BF16), pltpu.VMEM((NX, NY * 16, HALF), BF16),
            pltpu.VMEM((NY, 16, HALF), BF16), pltpu.VMEM((NY, 16, HALF), BF16),
            pltpu.VMEM((16, HALF), F32), pltpu.VMEM((16, HALF), F32),
            every(), every(), one(), one(),
            pltpu.VMEM((1, EDGES), I32),
            pltpu.VMEM((EDGES, HALF), BF16), pltpu.VMEM((EDGES, HALF), BF16),
            pltpu.VMEM((6, TILE, TILE), I32),
            pltpu.SemaphoreType.DMA, pltpu.SemaphoreType.DMA,
            dma(NX), dma(NX), dma(NY), dma(NY),
            pltpu.SemaphoreType.DMA, pltpu.SemaphoreType.DMA,
            pltpu.SemaphoreType.DMA, pltpu.SemaphoreType.DMA,
            dma(NX), dma(NX), dma(NZ), dma(NZ), dma(NY), dma(NY), dma(NX), dma(NX),
            dma(32), dma(32), dma(2), dma(2),
            pltpu.SemaphoreType.DMA, pltpu.SemaphoreType.DMA,
        ],
        compiler_params=pltpu.CompilerParams(
            collective_id=1, has_side_effects=True, vmem_limit_bytes=40 * 1024 * 1024
        ),
        name="atoms",
    )(partial, mid, source, target, atom_h, atom_gain.reshape(1, ATOM_WIDTH), w_atom, w_src, w_tgt)
    return edge_out, atom_out


def solution(mesh):
    placed = (
        P(("wide", "narrow"), None),
        P(("wide", "narrow"), None),
        P("narrow", None),
        P(("wide", "narrow")),
        P(("wide", "narrow")),
        P(("wide", "narrow"), None),
        P(("wide", "narrow"), None),
        P(), P(), P(), P(), P(), P(), P(), P(),
    )
    return jax.shard_map(
        per_device,
        mesh=mesh,
        in_specs=placed,
        out_specs=(P(("wide", "narrow"), None), P("narrow", None)),
        check_vma=False,
    )
```

time: 211 us -> 99.5 us (0.47)
  waiting for transfers between devices: 97.5 us -> 0 us
  Pallas kernels: 0 us -> 90.8 us
  local copies, waits for them, and re-layouts: 43.8 us -> 7.66 us
  blocking collectives: 23.6 us -> 0 us
  starting transfers between devices: 17.8 us -> 0 us
  between operations: 14.3 us -> 0.79 us
  matrix products: 12.6 us -> 0 us
    pallas_call x0 -> x2, Pallas kernels: none -> 90.8 us  [the longest x1 53.7 us: per_device(): pl.pallas_call(atom_kernel, out_shape=(jax.ShapeDtypeStruct((EDGES, WIDTH...]
    all_gather x1 -> x0, waiting for transfers between devices: 58.5 us -> none  [per_device(): every_atom = lax.all_gather(atom_out, 'narrow', axis=0, tiled=True)]
    gather x3 -> x0, local copies, waits for them, and re-layouts: 39.4 us -> none  [the longest x1 29.2 us: per_device(): other = received[trip_slot]]
    all_to_all x2 -> x0, waiting for transfers between devices: 39 us -> none  [the longest x1 28.5 us: sent_and_summed(): lax.all_to_all(pieces, axis, split_axis=0, concat_axis=0, tiled=True)]
    all_to_all x1 -> x0, blocking collectives: 23.6 us -> none  [copy_for_each(): return lax.all_to_all(copies, axis, split_axis=0, concat_axis=0, tiled=True)]
    all_to_all x2 -> x0, starting transfers between devices: 17.8 us -> none  [the longest x1 11.6 us: per_device(): lax.all_to_all(outgoing, 'wide', split_axis=0, concat_axis=0, tiled=True)]
    dot_general x7 -> x0, matrix products: 12.6 us -> none  [the longest x1 3.15 us: per_device(): jnp.dot(target_rows, w_tgt, preferred_element_type=jnp.float32)]
    unnamed x22 -> x29, local copies, waits for them, and re-layouts: 0.98 us -> 7.66 us
  transfers between devices with their start and end apart: 3 -> 0, of which waited for: 3 -> 0; matrix products, arithmetic and copies ran while one was open for 1% -> 0% of each run, Pallas kernels for 0% -> 0%
where the time goes in v1:
time: 99.5 us; the launch traced here: 99.2 us
  Pallas kernels  90.8 us (91%)
  local copies, waits for them, and re-layouts  7.66 us (8%)
    pallas_call x1, Pallas kernels, per_device(): pl.pallas_call(atom_kernel, out_shape=(jax.ShapeDtypeStruct((EDGES, WIDTH...  53.7 us
    pallas_call x1, Pallas kernels, per_device(): pl.pallas_call(mix_kernel, out_shape=(jax.ShapeDtypeStruct((EDGES, WIDTH)...  37.1 us
    unnamed x29, local copies, waits for them, and re-layouts  7.66 us

profile of v1, /device:TPU:1, one launch (start us, length us, event | category | flops | bytes accessed | tf_op | source)
XLA Modules:
  0.0 99.2 jit_solution(2213563502407894379)
XLA Ops:
  0.6 0.0 copy-start.3
  0.6 0.9 copy.17.slot_ref
  1.6 0.0 copy-start.8
  1.6 0.0 copy-start.9
  1.6 1.1 %copy.18.w_down_ref = bf16[1024,64]{1,0:T(8,128)(2,1)S(1)} copy(bf16[1024,64]{0,1:T(8,128)(2,1)} %param.22) | data formatting | bytes 262144 | tf_op args[7]
  2.7 0.0 copy-start.6
  2.7 0.0 copy-start.7
  2.7 1.1 %copy.19.w_bil_ref = bf16[1024,64]{1,0:T(8,128)(2,1)S(1)} copy(bf16[1024,64]{0,1:T(8,128)(2,1)} %param.23) | data formatting | bytes 262144 | tf_op args[8]
  3.8 0.0 copy-done.3
  3.8 0.0 copy-done.8
  3.8 0.0 copy-done.9
  3.8 0.0 copy-done.6
  3.9 0.0 copy-done.7
  3.9 0.0 copy-start
  3.9 1.2 %copy-done = bf16[1024,512]{1,0:T(8,128)(2,1)S(1)} copy-done((bf16[1024,512]{1,0:T(8,128)(2,1)S(1)}, bf16[1024,512]{1,0:T(8,128)(2,1)}, u32[]{:S(2)}) %copy-start) | copy-done | bytes 1048600
  5.1 0.0 copy-start.1
  5.1 0.0 copy-start.2
  5.1 0.0 copy-start.4
  5.1 37.1 %mix.1 = (bf16[256,1024]{1,0:T(8,128)(2,1)S(1)}, f32[512,512]{1,0:T(8,128)S(1)}) custom-call(bf16[256,1024]{1,0:T(8,128)(2,1)S(1)} %copy-done.3, bf16[256,512]{1,0:T(8,128)(2,1)S(1)} %copy-done.6, s32[256,32]{1,0:T(8,128)S(1)} %copy.17.slot_ref, s32[1,2048]{1,0:T(1,128)S(1)} %copy-done.8, s32[1,256]{1,0:T(1,128)S(1)} %bitcast.3, ...), custom_call_target="tpu_custom_call" | custom-call | tf_op jit(solution)/shard_map/mix/pallas_call | solution.py:327
  42.2 0.0 copy-start.10
  42.2 0.0 copy-start.11
  42.2 0.0 copy-done.1
  42.2 0.0 copy-done.2
  42.3 0.0 copy-done.4
  42.3 0.6 copy-done.10
  42.9 0.0 copy-done.11
  42.9 0.0 copy-start.5
  42.9 1.0 %copy-done.5 = bf16[512,512]{1,0:T(8,128)(2,1)S(1)} copy-done((bf16[512,512]{1,0:T(8,128)(2,1)S(1)}, bf16[512,512]{1,0:T(8,128)(2,1)}, u32[]{:S(2)}) %copy-start.5) | copy-done | bytes 524312
  44.0 53.7 %atoms.1 = (bf16[256,1024]{1,0:T(8,128)(2,1)S(1)}, bf16[512,512]{1,0:T(8,128)(2,1)S(1)}) custom-call(f32[512,512]{1,0:T(8,128)S(1)} %get-tuple-element.4.part_ref, bf16[256,1024]{1,0:T(8,128)(2,1)S(1)} %get-tuple-element.5.mid_ref, s32[1,256]{1,0:T(1,128)S(1)} %bitcast.6, s32[1,256]{1,0:T(1,128)S(1)} %bitcast.4, bf16[512,512]{1,0:T(8,128)(2,1)S(1)} %copy-done.4, ...), custom_call_target="tpu_custom_call" | custom-call | tf_op jit(solution)/shard_map/atoms/pallas_call | solution.py:359
  97.7 0.8 copy.22
  98.5 0.8 copy.23
Async XLA Ops:
  0.6 3.2 %copy-start.3 = (bf16[256,1024]{1,0:T(8,128)(2,1)S(1)}, bf16[256,1024]{1,0:T(8,128)(2,1)}, u32[]{:S(2)}) copy-start(bf16[256,1024]{1,0:T(8,128)(2,1)} %msg_ref.1) | copy-start | bytes 1572868
  1.6 2.3 %copy-start.8 = (s32[1,2048]{1,0:T(1,128)S(1)}, s32[1,2048]{1,0:T(1,128)}, u32[]{:S(2)}) copy-start(s32[1,2048]{1,0:T(1,128)} %rows_ref.1) | copy-start | bytes 24580
  1.6 2.3 %copy-start.9 = (s32[256]{0:T(256)S(1)}, s32[256]{0:T(256)}, u32[]{:S(2)}) copy-start(s32[256]{0:T(256)} %param.19) | copy-start | bytes 3076
  2.7 1.2 %copy-start.6 = (bf16[256,512]{1,0:T(8,128)(2,1)S(1)}, bf16[256,512]{1,0:T(8,128)(2,1)}, u32[]{:S(2)}) copy-start(bf16[256,512]{1,0:T(8,128)(2,1)} %basis_ref.1) | copy-start | bytes 786436
  2.7 1.2 %copy-start.7 = (bf16[64,1024]{1,0:T(8,128)(2,1)S(1)}, bf16[64,1024]{1,0:T(8,128)(2,1)}, u32[]{:S(2)}) copy-start(bf16[64,1024]{1,0:T(8,128)(2,1)} %w_up_ref.1) | copy-start | bytes 393220
  3.9 1.2 %copy-start = (bf16[1024,512]{1,0:T(8,128)(2,1)S(1)}, bf16[1024,512]{1,0:T(8,128)(2,1)}, u32[]{:S(2)}) copy-start(bf16[1024,512]{1,0:T(8,128)(2,1)} %w_in_ref.1) | copy-start | bytes 3145732
  5.1 37.1 %copy-start.1 = (bf16[512,1024]{1,0:T(8,128)(2,1)S(1)}, bf16[512,1024]{1,0:T(8,128)(2,1)}, u32[]{:S(2)}) copy-start(bf16[512,1024]{1,0:T(8,128)(2,1)} %w_src_ref.1) | copy-start | bytes 3145732
  5.1 37.2 %copy-start.2 = (bf16[512,1024]{1,0:T(8,128)(2,1)S(1)}, bf16[512,1024]{1,0:T(8,128)(2,1)}, u32[]{:S(2)}) copy-start(bf16[512,1024]{1,0:T(8,128)(2,1)} %w_tgt_ref.1) | copy-start | bytes 3145732
  5.1 37.2 %copy-start.4 = (bf16[512,512]{1,0:T(8,128)(2,1)S(1)}, bf16[512,512]{1,0:T(8,128)(2,1)}, u32[]{:S(2)}) copy-start(bf16[512,512]{1,0:T(8,128)(2,1)} %atom_ref.1) | copy-start | bytes 1572868
  42.2 0.7 copy-start.10
  42.2 0.7 copy-start.11
  42.9 1.0 %copy-start.5 = (bf16[512,512]{1,0:T(8,128)(2,1)S(1)}, bf16[512,512]{1,0:T(8,128)(2,1)}, u32[]{:S(2)}) copy-start(bf16[512,512]{1,0:T(8,128)(2,1)} %w_atom_ref.1) | copy-start | bytes 1572868

commit v2 on v1

v2 whole, which is shorter than its diff:
```python
import jax
import jax.numpy as jnp
from jax import lax
from jax.experimental import pallas as pl
from jax.experimental.pallas import tpu as pltpu
from jax.sharding import PartitionSpec as P

MESH = pl.DeviceIdType.MESH
BF16, F32, I32 = jnp.bfloat16, jnp.float32, jnp.int32
NX, NY, NZ = 4, 8, 8
WIDE = NX * NY * 2
EDGES, WIDTH, TRIP, BASIS, TRIPLETS, SLOTS = 256, 1024, 64, 16, 32, 32
ATOMS, ATOM_WIDTH, HALF, TILE = 512, 512, 256, 128
GROUP = 32


def silu(value):
    return value / (1.0 + jnp.exp(-value))


def dot(a, b):
    return jnp.dot(a, b, preferred_element_type=F32)


def iota(shape, dim):
    return lax.broadcasted_iota(I32, shape, dim)


def dot_t(a, b):
    return lax.dot_general(a, b, (((1,), (1,)), ((), ())), preferred_element_type=F32)


def ones_where(mask):
    return jnp.where(mask, 1.0, 0.0).astype(BF16)


def remote(src, dst, send_sem, recv_sem, device):
    return pltpu.make_async_remote_copy(
        src_ref=src, dst_ref=dst, send_sem=send_sem, recv_sem=recv_sem,
        device_id=device, device_id_type=MESH,
    )


def kernel(
    source_ref, target_ref, gain_ref, msg_hbm, rows_hbm, w_down_hbm, basis_hbm, slot_hbm, w_bil_hbm, w_up_hbm,
    w_in_hbm, w_src_hbm, w_tgt_hbm, w_atom_hbm, atom_hbm,
    edge_out, atom_out,
    msg_ref, rows_ref, w_down_ref, basis_ref, slot_ref, w_bil_ref, w_up_ref, w_in_ref, w_src_ref, w_tgt_ref,
    w_atom_ref, atom_ref, load_sem,
    out_buf, in_buf, table, spread, bands, digit_buf, where_buf, mixed, send_sem, recv_sem, mid_ref, part_ref,
    snd1, rcv1, snd2, rcv2, snd3, rcv3, snd4, rcv4, all_a, all_b, sib_a, sib_b, src_sib, pick_snd, pick_rcv, col,
    s1, r1, s2, r2, s3, r3, s4, r4, si, ri, sa1, ra1, sb1, rb1, sa2, ra2, sb2, rb2, sring, rring, so, ro, sp, rp,
):
    me, row = lax.axis_index("wide"), lax.axis_index("narrow")
    x, y, c, z = me // 16, (me // 2) % NY, me % 2, row
    other = 1 - c
    barrier = pltpu.get_barrier_semaphore()

    def at(px, py, pc, pz):
        return (px * 16 + py * 2 + pc, pz)

    sibling = at(x, y, other, z)
    xs = [(lax.rem(x + i, NX), i) for i in range(1, NX)]
    ys = [(lax.rem(y + i, NY), i) for i in range(1, NY)]
    zs = [(lax.rem(z + i, NZ), i) for i in range(1, NZ)]
    waiting = []

    def start(copy):
        copy.start()
        waiting.append(copy)

    def greet(i, carry):
        pl.semaphore_signal(barrier, inc=1, device_id=(lax.rem(me + i, WIDE), row), device_id_type=MESH)
        return carry

    lax.fori_loop(1, WIDE, greet, 0)
    for p, _ in zs:
        pl.semaphore_signal(barrier, inc=1, device_id=at(x, y, c, p), device_id_type=MESH)

    mine, theirs = pl.ds(pl.multiple_of(c * HALF, HALF), HALF), pl.ds(pl.multiple_of(other * HALF, HALF), HALF)
    my_rows = pl.ds(pl.multiple_of(x * TILE + y * 16, 16), 16)
    pairs = [
        (msg_hbm, msg_ref), (w_down_hbm, w_down_ref), (rows_hbm, rows_ref), (basis_hbm, basis_ref),
        (slot_hbm, slot_ref), (w_bil_hbm, w_bil_ref), (w_up_hbm, w_up_ref), (w_in_hbm, w_in_ref),
        (w_atom_hbm.at[:, mine], w_atom_ref), (atom_hbm.at[my_rows, mine], atom_ref),
        (w_src_hbm, w_src_ref), (w_tgt_hbm, w_tgt_ref),
    ]
    loads = [pltpu.make_async_copy(a, b, load_sem.at[i]) for i, (a, b) in enumerate(pairs)]
    for load in loads:
        load.start()
    for load in loads[:3]:
        load.wait()

    down = silu(dot_t(w_down_ref[...], msg_ref[...]))
    twice = jnp.concatenate([down, down], axis=0).astype(BF16)
    low_lane = iota((16, TILE), 1) < TRIP
    for j in range(8):
        hot = ones_where(iota((EDGES, 256), 0) == rows_ref[:, j * 256 : (j + 1) * 256])
        picked = dot(twice, hot).T
        for p in range(8):
            first, second = picked[p * 32 : p * 32 + 16], picked[p * 32 + 16 : p * 32 + 32]
            out_buf[j * 8 + p] = jnp.where(low_lane, first, second).astype(BF16)

    pl.semaphore_wait(barrier, WIDE - 1 + NZ - 1)
    start(remote(source_ref, src_sib, si, ri, sibling))
    def copy_to(i):
        peer = lax.rem(me + i, WIDE)
        return peer, remote(out_buf.at[peer], in_buf.at[me], send_sem.at[peer], recv_sem.at[me], (peer, row))

    def send(i, carry):
        copy_to(i)[1].start()
        return carry

    lax.fori_loop(1, WIDE, send, 0)
    in_buf[me] = out_buf[me]

    for load in loads[3:5]:
        load.wait()
    spread[...] = ones_where((iota((512, 256), 0) >> 4) == (iota((512, 256), 1) & 31))
    key = iota((8, 512), 1) & 15
    band = (iota((TILE, 256), 0) & 7) == (iota((TILE, 256), 1) >> 5)

    def build(i, carry):
        two = basis_ref[pl.ds(pl.multiple_of(i * 16, 16), 16), :].astype(F32)
        for h in range(2):
            x = two[h * 8 : h * 8 + 8]
            tall = jnp.concatenate([jnp.where(key == k, x, 0.0) for k in range(BASIS)], axis=0)
            block = jnp.where(band, dot(tall.astype(BF16), spread[...]), 0.0)
            bands[pl.ds(pl.multiple_of(i * 256 + h * TILE, TILE), TILE), :] = block.astype(BF16)
        return carry

    lax.fori_loop(0, EDGES // 16, build, 0, unroll=2)

    slots = slot_ref[...]
    parts = [(slots >> 5) & 31, slots & 15, ((slots >> 10) << 1) | ((slots >> 4) & 1), slots * 0]
    digits = jnp.concatenate(parts, axis=0).astype(F32).T
    digit = iota((TILE, 256), 0) >> 5
    left = iota((TILE, 256), 1) < TILE
    weigh = jnp.where(left & (digit == 0), 16.0, jnp.where(digit == jnp.where(left, 1, 2), 1.0, 0.0)).astype(BF16)
    own_digit = (iota((TRIPLETS, TILE), 1) & 31) == iota((TRIPLETS, TILE), 0)
    digit_buf[...] = digits

    def place(i, carry):
        few = digit_buf[pl.ds(pl.multiple_of(i * 8, 8), 8), :]
        tall = [jnp.where(own_digit, few[e : e + 1], 0.0) for e in range(8)]
        where_buf[pl.ds(pl.multiple_of(i * 256, 256), 256), :] = dot(
            jnp.concatenate(tall, axis=0).astype(BF16), weigh
        )
        return carry

    lax.fori_loop(0, EDGES // 8, place, 0, unroll=2)

    remote(source_ref, src_sib, si, ri, sibling).wait_recv()
    for i, ref in enumerate((source_ref, src_sib, target_ref)):
        for h in range(2):
            line = ref[:, h * TILE : (h + 1) * TILE].astype(F32)
            turned = jnp.broadcast_to(line, (TILE, TILE)).T
            col[i * 2 + h] = turned.astype(I32)

    def arrived(i, carry):
        peer = lax.rem(me + i, WIDE)
        remote(out_buf.at[peer], in_buf.at[peer], send_sem.at[peer], recv_sem.at[peer], (peer, row)).wait_recv()
        return carry

    lax.fori_loop(1, WIDE, arrived, 0)

    received = in_buf[...].reshape(WIDE * 16, TILE)
    table[...] = jnp.concatenate([received[:512], received[512:]], axis=1)
    low_lane8 = iota((8, TILE), 1) < TRIP
    lane = iota((GROUP * TRIPLETS, TILE), 1).astype(F32)
    lane_half = (iota((GROUP * TRIPLETS, TILE), 1) >> 6).astype(F32)

    def mix(i, carry):
        lines = pl.ds(pl.multiple_of(i * GROUP * TRIPLETS, GROUP * TRIPLETS), GROUP * TRIPLETS)
        q, g = where_buf[lines, :TILE], where_buf[lines, TILE:]
        hot = jnp.concatenate([ones_where(q == lane + float(j * TILE)) for j in range(4)], axis=1)
        four = dot(hot, table[...])
        rows = jnp.where(g == lane_half, four[:, :TILE], 0.0) + jnp.where(g == lane_half + 2.0, four[:, TILE:], 0.0)
        rows = rows.astype(BF16)
        for b in range(GROUP // 8):
            block = bands[pl.ds(pl.multiple_of((i * (GROUP // 8) + b) * TILE, TILE), TILE), :]
            got = dot(block, rows[b * 256 : (b + 1) * 256])
            got = got + pltpu.roll(got, TRIP, 1)
            for k in range(8):
                pair = jnp.where(low_lane8, got[k * 16 : k * 16 + 8], got[k * 16 + 8 : k * 16 + 16])
                mixed[pl.ds(pl.multiple_of(i * GROUP + b * 8, 8), 8), k * TILE : (k + 1) * TILE] = pair
        return carry

    lax.fori_loop(0, EDGES // GROUP, mix, 0)

    for load in loads[5:]:
        load.wait()
    trip = silu(dot_t(mixed[...].astype(BF16), w_bil_ref[...])).astype(BF16)
    mid = (msg_ref[...].astype(F32) + dot(trip, w_up_ref[...])).astype(BF16)
    mid_ref[...] = mid
    message = dot(mid, w_in_ref[...]).astype(BF16)
    hot = ones_where(iota((ATOMS, EDGES), 0) == target_ref[...] - row * ATOMS)
    part_ref[...] = dot(hot, message)

    my_x = pl.ds(pl.multiple_of(x * TILE, TILE), TILE)
    order = [p for p, _ in xs] + [x]

    def chip_copy(i, p):
        return remote(snd1.at[i], rcv1.at[i], s1.at[i], r1.at[i], sibling)

    for i, p in enumerate(order):
        snd1[i] = part_ref[pl.ds(pl.multiple_of(p * TILE, TILE), TILE), theirs].astype(BF16)
        start(chip_copy(i, p))
    for i, p in enumerate(order):
        chip_copy(i, p).wait_recv()
        if i < NX - 1:
            rows = part_ref[pl.ds(pl.multiple_of(p * TILE, TILE), TILE), mine] + rcv1[i].astype(F32)
            snd2[i] = rows.astype(BF16)
            start(remote(snd2.at[i], rcv2.at[x], s2.at[i], r2.at[x], at(p, y, c, z)))
    total = part_ref[my_x, mine] + rcv1[NX - 1].astype(F32)
    for p, _ in xs:
        remote(snd2.at[0], rcv2.at[p], s2.at[0], r2.at[p], at(p, y, c, z)).wait_recv()
        total = total + rcv2[p].astype(F32)
    snd3[...] = total.astype(BF16).reshape(NY, 16, HALF)
    for p, _ in ys:
        start(remote(snd3.at[p], rcv3.at[y], s3.at[p], r3.at[y], at(x, p, c, z)))
    share = snd3[y].astype(F32)
    for p, _ in ys:
        remote(snd3.at[p], rcv3.at[p], s3.at[p], r3.at[p], at(x, p, c, z)).wait_recv()
        share = share + rcv3[p].astype(F32)
    snd4[...] = share
    start(remote(snd4, rcv4, s4, r4, sibling))


    remote(snd4, rcv4, s4, r4, sibling).wait_recv()
    theirs4 = rcv4[...]
    squares = jnp.sum(share * share, axis=-1, keepdims=True) + jnp.sum(theirs4 * theirs4, axis=-1, keepdims=True)
    scale = lax.rsqrt(squares * (1.0 / ATOM_WIDTH) + 1e-06)
    norm_mine = (share * scale * gain_ref[:, mine]).astype(BF16)
    norm_theirs = (theirs4 * scale * gain_ref[:, theirs]).astype(BF16)
    grown = silu(dot(norm_mine, w_atom_ref[mine, :]) + dot(norm_theirs, w_atom_ref[theirs, :]))
    fresh = (atom_ref[...].astype(F32) + grown).astype(BF16)
    all_a[z, x, y] = fresh[:, :TILE]
    all_b[z, x, y] = fresh[:, TILE:]

    for p, _ in xs:
        start(remote(all_a.at[z, x, y], all_a.at[z, x, y], sa1.at[p], ra1.at[x], at(p, y, c, z)))
    for p, _ in zs:
        start(remote(all_b.at[z, x, y], all_b.at[z, x, y], sb1.at[p], rb1.at[z], at(x, y, c, p)))
    for p, _ in xs:
        block = all_a.at[z, p, y]
        remote(block, block, sa1.at[p], ra1.at[p], at(p, y, c, z)).wait_recv()
    for p, _ in ys:
        block = all_a.at[z, :, y]
        start(remote(block, block, sa2.at[p], ra2.at[y], at(x, p, c, z)))
    for p, _ in zs:
        block = all_b.at[p, x, y]
        remote(block, block, sb1.at[p], rb1.at[p], at(x, y, c, p)).wait_recv()
    for p, _ in xs:
        block = all_b.at[:, x, y]
        start(remote(block, block, sb2.at[p], rb2.at[x], at(p, y, c, z)))

    def ring_copy(axis, way, step, part, sending):
        n, pos = (NZ, z) if axis == 0 else (NY, y)
        hop = 1 if way == 0 else n - 1
        back = step - 1 if sending else step
        block = lax.rem(pos + (n - back if way == 0 else back), n)
        view = all_a.at[block, part] if axis == 0 else all_b.at[:, part, block]
        to = lax.rem(pos + hop, n)
        device = at(x, y, c, to) if axis == 0 else at(x, to, c, z)
        index = ((axis * 2 + way) * 4 + step - 1) * NX + part
        return remote(view, view, sring.at[index], rring.at[index], device)

    for p, _ in xs:
        block = all_b.at[:, p, y]
        remote(block, block, sb2.at[p], rb2.at[p], at(p, y, c, z)).wait_recv()
    for part in range(NX):
        for way in range(2):
            start(ring_copy(1, way, 1, part, True))
    for p, _ in ys:
        block = all_a.at[z, :, p]
        remote(block, block, sa2.at[p], ra2.at[p], at(x, p, c, z)).wait_recv()
    for part in range(NX):
        for way in range(2):
            start(ring_copy(0, way, 1, part, True))
    own_a = remote(all_a.at[z], sib_a, so.at[0], ro.at[0], sibling)
    start(own_a)
    for step in range(1, 5):
        for part in range(NX):
            for axis in (1, 0):
                for way in range(2):
                    last = part // 2 == way
                    if step == 4 and not last:
                        continue
                    ring_copy(axis, way, step, part, False).wait_recv()
                    if step < 3 or (step == 3 and last):
                        start(ring_copy(axis, way, step + 1, part, True))
    own_b = remote(all_b.at[z], sib_b, so.at[1], ro.at[1], sibling)
    start(own_b)

    lanes = iota((EDGES, ATOMS), 1)

    def column(i):
        halves = [jnp.concatenate([col[i * 2 + h]] * (ATOMS // TILE), axis=1) for h in range(2)]
        return jnp.concatenate(halves, axis=0)

    def rows_of(first_ref, second_ref):
        a, b = first_ref[...].reshape(ATOMS, TILE), second_ref[...].reshape(ATOMS, TILE)
        return jnp.concatenate([a, b], axis=1)

    def picked(i):
        total = jnp.zeros((EDGES, HALF), F32)
        for block in range(NZ):
            hot = ones_where(column(i) - block * ATOMS == lanes)
            total = total + dot(hot, rows_of(all_a.at[block], all_b.at[block]))
        return total.astype(BF16)

    pick_snd[...] = picked(1)
    start(remote(pick_snd, pick_rcv, sp, rp, sibling))
    update = dot(picked(0), w_src_ref[mine, :])
    own_a.wait_recv()
    own_b.wait_recv()
    hot = ones_where(column(2) - z * ATOMS == lanes)
    ours = rows_of(all_a.at[z], all_b.at[z])
    sibs = rows_of(sib_a, sib_b)
    atom_out[:, mine] = ours
    atom_out[:, theirs] = sibs
    update += dot(dot(hot, ours).astype(BF16), w_tgt_ref[mine, :])
    update += dot(dot(hot, sibs).astype(BF16), w_tgt_ref[theirs, :])
    remote(pick_snd, pick_rcv, sp, rp, sibling).wait_recv()
    update += dot(pick_rcv[...], w_src_ref[theirs, :])
    edge_out[...] = (mid_ref[...].astype(F32) + silu(update)).astype(BF16)
    for copy in waiting:
        copy.wait_send()

    def sent(i, carry):
        copy_to(i)[1].wait_send()
        return carry

    lax.fori_loop(1, WIDE, sent, 0)


def dma(*shape):
    return pltpu.SemaphoreType.DMA(shape)


def per_device(
    edge_msg, basis, atom_h, edge_source, edge_target, send_rows, trip_slot,
    w_down, w_bil, w_up, w_atom_in, atom_gain, w_atom, w_src, w_tgt,
):
    vmem = pl.BlockSpec(memory_space=pltpu.VMEM)
    hbm = pl.BlockSpec(memory_space=pltpu.HBM)

    def every():
        return pltpu.VMEM((NZ, NX, NY, 16, TILE), BF16)

    def one():
        return pltpu.VMEM((NX, NY, 16, TILE), BF16)

    def semaphores(n):
        return [pltpu.SemaphoreType.DMA] * n

    edge_out, atom_out = pl.pallas_call(
        kernel,
        out_shape=(
            jax.ShapeDtypeStruct((EDGES, WIDTH), BF16),
            jax.ShapeDtypeStruct((ATOMS, ATOM_WIDTH), BF16),
        ),
        in_specs=[vmem] * 3 + [hbm] * 12,
        out_specs=(vmem, vmem),
        scratch_shapes=[
            pltpu.VMEM((EDGES, WIDTH), BF16),
            pltpu.VMEM((1, WIDE * SLOTS), I32),
            pltpu.VMEM((TRIP, WIDTH), BF16),
            pltpu.VMEM((EDGES, TRIPLETS * BASIS), BF16),
            pltpu.VMEM((TRIPLETS, EDGES), I32),
            pltpu.VMEM((TRIP, BASIS * TRIP), BF16),
            pltpu.VMEM((TRIP, WIDTH), BF16),
            pltpu.VMEM((WIDTH, ATOM_WIDTH), BF16),
            pltpu.VMEM((ATOM_WIDTH, WIDTH), BF16),
            pltpu.VMEM((ATOM_WIDTH, WIDTH), BF16),
            pltpu.VMEM((ATOM_WIDTH, HALF), BF16),
            pltpu.VMEM((16, HALF), BF16),
            dma(12),
            pltpu.VMEM((WIDE, 16, TILE), BF16),
            pltpu.VMEM((WIDE, 16, TILE), BF16),
            pltpu.VMEM((512, 256), BF16),
            pltpu.VMEM((512, 256), BF16),
            pltpu.VMEM((EDGES * BASIS, 256), BF16),
            pltpu.VMEM((EDGES, TILE), F32),
            pltpu.VMEM((EDGES * TRIPLETS, 256), F32),
            pltpu.VMEM((EDGES, BASIS * TRIP), F32),
            dma(WIDE),
            dma(WIDE),
            pltpu.VMEM((EDGES, WIDTH), BF16),
            pltpu.VMEM((ATOMS, ATOM_WIDTH), F32),
            pltpu.VMEM((NX, TILE, HALF), BF16), pltpu.VMEM((NX, TILE, HALF), BF16),
            pltpu.VMEM((NX, NY * 16, HALF), BF16), pltpu.VMEM((NX, NY * 16, HALF), BF16),
            pltpu.VMEM((NY, 16, HALF), BF16), pltpu.VMEM((NY, 16, HALF), BF16),
            pltpu.VMEM((16, HALF), F32), pltpu.VMEM((16, HALF), F32),
            every(), every(), one(), one(),
            pltpu.VMEM((1, EDGES), I32),
            pltpu.VMEM((EDGES, HALF), BF16), pltpu.VMEM((EDGES, HALF), BF16),
            pltpu.VMEM((6, TILE, TILE), I32),
            dma(NX), dma(NX), dma(NX), dma(NX), dma(NY), dma(NY),
            *semaphores(4),
            dma(NX), dma(NX), dma(NZ), dma(NZ), dma(NY), dma(NY), dma(NX), dma(NX),
            dma(64), dma(64), dma(2), dma(2),
            *semaphores(2),
        ],
        compiler_params=pltpu.CompilerParams(
            collective_id=0, has_side_effects=True, vmem_limit_bytes=60 * 1024 * 1024
        ),
        name="block",
    )(
        edge_source.reshape(1, EDGES), edge_target.reshape(1, EDGES), atom_gain.reshape(1, ATOM_WIDTH),
        edge_msg, send_rows, w_down.T, basis, trip_slot.T, w_bil.T, w_up, w_atom_in, w_src, w_tgt, w_atom, atom_h,
    )
    return edge_out, atom_out


def solution(mesh):
    placed = (
        P(("wide", "narrow"), None),
        P(("wide", "narrow"), None),
        P("narrow", None),
        P(("wide", "narrow")),
        P(("wide", "narrow")),
        P(("wide", "narrow"), None),
        P(("wide", "narrow"), None),
        P(), P(), P(), P(), P(), P(), P(), P(),
    )
    return jax.shard_map(
        per_device,
        mesh=mesh,
        in_specs=placed,
        out_specs=(P(("wide", "narrow"), None), P("narrow", None)),
        check_vma=False,
    )
```

time: 99.5 us -> 83.6 us (0.84)
  Pallas kernels: 90.8 us -> 79.6 us
  local copies, waits for them, and re-layouts: 7.66 us -> 2.72 us
    pallas_call x2 -> x1, Pallas kernels: 90.8 us -> 79.6 us  [per_device(): pl.pallas_call(kernel, out_shape=(jax.ShapeDtypeStruct((EDGES, WIDTH), BF...]
    unnamed x29 -> x4, local copies, waits for them, and re-layouts: 7.66 us -> 2.72 us
where the time goes in v2:
time: 83.6 us; the launch traced here: 83 us
  Pallas kernels  79.6 us (95%)
  local copies, waits for them, and re-layouts  2.72 us (3%)
    pallas_call x1, Pallas kernels, per_device(): pl.pallas_call(kernel, out_shape=(jax.ShapeDtypeStruct((EDGES, WIDTH), BF...  79.6 us
    unnamed x4, local copies, waits for them, and re-layouts  2.72 us

profile of v2, /device:TPU:1, one launch (start us, length us, event | category | flops | bytes accessed | tf_op | source)
XLA Modules:
  0.0 83.0 jit_solution(16146886486052011670)
XLA Ops:
  0.6 79.6 %block.1 = (bf16[256,1024]{1,0:T(8,128)(2,1)}, bf16[512,512]{1,0:T(8,128)(2,1)}) custom-call(s32[1,256]{1,0:T(1,128)} %bitcast.10, s32[1,256]{1,0:T(1,128)} %bitcast.11, f32[1,512]{1,0:T(1,128)} %bitcast.9, bf16[256,1024]{1,0:T(8,128)(2,1)} %msg_hbm.1, s32[1,2048]{1,0:T(1,128)} %rows_hbm.1, bf16[64,1024]{1,0:T(8,128)(2,1)} %bitcast.6, ...), custom_call_target="tpu_custom_call" | custom-call | tf_op jit(solution)/shard_map/block/pallas_call | solution.py:358
  80.2 0.0 copy-start
  80.2 1.9 %copy.19 = bf16[256,1024]{1,0:T(8,128)(2,1)} copy(bf16[256,1024]{1,0:T(8,128)(2,1)} %get-tuple-element.4) | data formatting | bytes 1048576
  82.2 0.0 copy-done
  82.2 0.8 copy.20
Async XLA Ops:
  80.2 1.9 %copy-start = (bf16[512,512]{1,0:T(8,128)(2,1)S(1)}, bf16[512,512]{1,0:T(8,128)(2,1)}, u32[]{:S(2)}) copy-start(bf16[512,512]{1,0:T(8,128)(2,1)} %get-tuple-element.5) | copy-start | bytes 1572868

commit v3 on v2

--- a/solution.py
+++ b/solution.py
@@ -47,9 +47,9 @@
     edge_out, atom_out,
     msg_ref, rows_ref, w_down_ref, basis_ref, slot_ref, w_bil_ref, w_up_ref, w_in_ref, w_src_ref, w_tgt_ref,
     w_atom_ref, atom_ref, load_sem,
-    out_buf, in_buf, table, spread, bands, digit_buf, where_buf, mixed, send_sem, recv_sem, mid_ref, part_ref,
+    out_buf, in_buf, table, spread, bands, digit_buf, group_buf, hot_buf, mixed, send_sem, recv_sem, mid_ref, part_ref,
     snd1, rcv1, snd2, rcv2, snd3, rcv3, snd4, rcv4, all_a, all_b, sib_a, sib_b, src_sib, pick_snd, pick_rcv, col,
-    s1, r1, s2, r2, s3, r3, s4, r4, si, ri, sa1, ra1, sb1, rb1, sa2, ra2, sb2, rb2, sring, rring, so, ro, sp, rp,
+    s1, r1, s2, r2, s3, r3, s4, r4, si, ri, sa1, ra1, sb1, rb1, sring, rring, sfar, rfar, sshare, rshare, so, ro, sp, rp,
 ):
     me, row = lax.axis_index("wide"), lax.axis_index("narrow")
     x, y, c, z = me // 16, (me // 2) % NY, me % 2, row
@@ -63,19 +63,16 @@
     xs = [(lax.rem(x + i, NX), i) for i in range(1, NX)]
     ys = [(lax.rem(y + i, NY), i) for i in range(1, NY)]
     zs = [(lax.rem(z + i, NZ), i) for i in range(1, NZ)]
+    place_a, place_b = x * NY + y, x * NZ + z
     waiting = []
 
     def start(copy):
         copy.start()
         waiting.append(copy)
 
-    def greet(i, carry):
-        pl.semaphore_signal(barrier, inc=1, device_id=(lax.rem(me + i, WIDE), row), device_id_type=MESH)
-        return carry
-
-    lax.fori_loop(1, WIDE, greet, 0)
-    for p, _ in zs:
-        pl.semaphore_signal(barrier, inc=1, device_id=at(x, y, c, p), device_id_type=MESH)
+    def drain(keep):
+        while len(waiting) > keep:
+            waiting.pop(0).wait_send()
 
     mine, theirs = pl.ds(pl.multiple_of(c * HALF, HALF), HALF), pl.ds(pl.multiple_of(other * HALF, HALF), HALF)
     my_rows = pl.ds(pl.multiple_of(x * TILE + y * 16, 16), 16)
@@ -88,6 +85,15 @@
     loads = [pltpu.make_async_copy(a, b, load_sem.at[i]) for i, (a, b) in enumerate(pairs)]
     for load in loads:
         load.start()
+
+    def greet(i, carry):
+        pl.semaphore_signal(barrier, inc=1, device_id=(lax.rem(me + i, WIDE), row), device_id_type=MESH)
+        return carry
+
+    lax.fori_loop(1, WIDE, greet, 0)
+    for px in range(NX):
+        for p, _ in zs:
+            pl.semaphore_signal(barrier, inc=1, device_id=at(px, y, c, p), device_id_type=MESH)
     for load in loads[:3]:
         load.wait()
 
@@ -101,7 +107,7 @@
             first, second = picked[p * 32 : p * 32 + 16], picked[p * 32 + 16 : p * 32 + 32]
             out_buf[j * 8 + p] = jnp.where(low_lane, first, second).astype(BF16)
 
-    pl.semaphore_wait(barrier, WIDE - 1 + NZ - 1)
+    pl.semaphore_wait(barrier, WIDE - 1 + NX * (NZ - 1))
     start(remote(source_ref, src_sib, si, ri, sibling))
     def copy_to(i):
         peer = lax.rem(me + i, WIDE)
@@ -139,13 +145,16 @@
     weigh = jnp.where(left & (digit == 0), 16.0, jnp.where(digit == jnp.where(left, 1, 2), 1.0, 0.0)).astype(BF16)
     own_digit = (iota((TRIPLETS, TILE), 1) & 31) == iota((TRIPLETS, TILE), 0)
     digit_buf[...] = digits
+    lane = iota((256, TILE), 1).astype(F32)
 
     def place(i, carry):
         few = digit_buf[pl.ds(pl.multiple_of(i * 8, 8), 8), :]
         tall = [jnp.where(own_digit, few[e : e + 1], 0.0) for e in range(8)]
-        where_buf[pl.ds(pl.multiple_of(i * 256, 256), 256), :] = dot(
-            jnp.concatenate(tall, axis=0).astype(BF16), weigh
-        )
+        found = dot(jnp.concatenate(tall, axis=0).astype(BF16), weigh)
+        lines = pl.ds(pl.multiple_of(i * 256, 256), 256)
+        hot = [ones_where(found[:, :TILE] == lane + float(j * TILE)) for j in range(4)]
+        hot_buf[lines, :] = jnp.concatenate(hot, axis=1)
+        group_buf[lines, :] = found[:, TILE:]
         return carry
 
     lax.fori_loop(0, EDGES // 8, place, 0, unroll=2)
@@ -167,14 +176,11 @@
     received = in_buf[...].reshape(WIDE * 16, TILE)
     table[...] = jnp.concatenate([received[:512], received[512:]], axis=1)
     low_lane8 = iota((8, TILE), 1) < TRIP
-    lane = iota((GROUP * TRIPLETS, TILE), 1).astype(F32)
     lane_half = (iota((GROUP * TRIPLETS, TILE), 1) >> 6).astype(F32)
 
     def mix(i, carry):
         lines = pl.ds(pl.multiple_of(i * GROUP * TRIPLETS, GROUP * TRIPLETS), GROUP * TRIPLETS)
-        q, g = where_buf[lines, :TILE], where_buf[lines, TILE:]
-        hot = jnp.concatenate([ones_where(q == lane + float(j * TILE)) for j in range(4)], axis=1)
-        four = dot(hot, table[...])
+        four, g = dot(hot_buf[lines, :], table[...]), group_buf[lines, :]
         rows = jnp.where(g == lane_half, four[:, :TILE], 0.0) + jnp.where(g == lane_half + 2.0, four[:, TILE:], 0.0)
         rows = rows.astype(BF16)
         for b in range(GROUP // 8):
@@ -206,6 +212,11 @@
     for i, p in enumerate(order):
         snd1[i] = part_ref[pl.ds(pl.multiple_of(p * TILE, TILE), TILE), theirs].astype(BF16)
         start(chip_copy(i, p))
+    def sent(i, carry):
+        copy_to(i)[1].wait_send()
+        return carry
+
+    lax.fori_loop(1, WIDE, sent, 0)
     for i, p in enumerate(order):
         chip_copy(i, p).wait_recv()
         if i < NX - 1:
@@ -238,22 +249,33 @@
     all_a[z, x, y] = fresh[:, :TILE]
     all_b[z, x, y] = fresh[:, TILE:]
 
-    for p, _ in xs:
-        start(remote(all_a.at[z, x, y], all_a.at[z, x, y], sa1.at[p], ra1.at[x], at(p, y, c, z)))
-    for p, _ in zs:
-        start(remote(all_b.at[z, x, y], all_b.at[z, x, y], sb1.at[p], rb1.at[z], at(x, y, c, p)))
-    for p, _ in xs:
-        block = all_a.at[z, p, y]
-        remote(block, block, sa1.at[p], ra1.at[p], at(p, y, c, z)).wait_recv()
-    for p, _ in ys:
-        block = all_a.at[z, :, y]
-        start(remote(block, block, sa2.at[p], ra2.at[y], at(x, p, c, z)))
-    for p, _ in zs:
-        block = all_b.at[p, x, y]
-        remote(block, block, sb1.at[p], rb1.at[p], at(x, y, c, p)).wait_recv()
-    for p, _ in xs:
-        block = all_b.at[:, x, y]
-        start(remote(block, block, sb2.at[p], rb2.at[x], at(p, y, c, z)))
+    def plane_copies(i, sending):
+        a, b = lax.rem(place_a + i, NX * NY), lax.rem(place_b + i, NX * NZ)
+        ax, ay, bx, bz = a // NY, a % NY, b // NZ, b % NZ
+        view_a = all_a.at[z, x, y] if sending else all_a.at[z, ax, ay]
+        view_b = all_b.at[z, x, y] if sending else all_b.at[bz, bx, y]
+        return (
+            remote(view_a, view_a, sa1.at[a], ra1.at[place_a if sending else a], at(ax, ay, c, z)),
+            remote(view_b, view_b, sb1.at[b], rb1.at[place_b if sending else b], at(bx, y, c, bz)),
+        )
+
+    def plane_send(i, carry):
+        for copy in plane_copies(i, True):
+            copy.start()
+        return carry
+
+    def plane_arrived(i, carry):
+        for copy in plane_copies(i, False):
+            copy.wait_recv()
+        return carry
+
+    def plane_sent(i, carry):
+        for copy in plane_copies(i, True):
+            copy.wait_send()
+        return carry
+
+    lax.fori_loop(1, NX * NY, plane_send, 0)
+    lax.fori_loop(1, NX * NY, plane_arrived, 0)
 
     def ring_copy(axis, way, step, part, sending):
         n, pos = (NZ, z) if axis == 0 else (NY, y)
@@ -266,30 +288,47 @@
         index = ((axis * 2 + way) * 4 + step - 1) * NX + part
         return remote(view, view, sring.at[index], rring.at[index], device)
 
-    for p, _ in xs:
-        block = all_b.at[:, p, y]
-        remote(block, block, sb2.at[p], rb2.at[p], at(p, y, c, z)).wait_recv()
+    across = lax.rem(z + 4, NZ), lax.rem(y + 4, NY)
+
+    def quarter(axis, block, part):
+        return all_a.at[block, part] if axis == 0 else all_b.at[:, part, block]
+
+    def far_copy(axis, sending):
+        view = quarter(axis, (z if axis == 0 else y) if sending else across[axis], x)
+        device = at(x, y, c, across[0]) if axis == 0 else at(x, across[1], c, z)
+        return remote(view, view, sfar.at[axis], rfar.at[axis], device)
+
+    def share_copy(axis, p, sending):
+        view = quarter(axis, across[axis], x if sending else p)
+        return remote(view, view, sshare.at[axis * NX + p], rshare.at[axis * NX + (x if sending else p)], at(p, y, c, z))
+
+    for axis in (1, 0):
+        start(far_copy(axis, True))
     for part in range(NX):
-        for way in range(2):
-            start(ring_copy(1, way, 1, part, True))
-    for p, _ in ys:
-        block = all_a.at[z, :, p]
-        remote(block, block, sa2.at[p], ra2.at[p], at(x, p, c, z)).wait_recv()
-    for part in range(NX):
-        for way in range(2):
-            start(ring_copy(0, way, 1, part, True))
+        for axis in (1, 0):
+            for way in range(2):
+                start(ring_copy(axis, way, 1, part, True))
     own_a = remote(all_a.at[z], sib_a, so.at[0], ro.at[0], sibling)
     start(own_a)
-    for step in range(1, 5):
+    lax.fori_loop(1, NX * NY, plane_sent, 0)
+    drain(19)
+    for step in range(1, 4):
         for part in range(NX):
             for axis in (1, 0):
                 for way in range(2):
-                    last = part // 2 == way
-                    if step == 4 and not last:
-                        continue
                     ring_copy(axis, way, step, part, False).wait_recv()
-                    if step < 3 or (step == 3 and last):
+                    if step < 3:
                         start(ring_copy(axis, way, step + 1, part, True))
+        if step == 1:
+            for axis in (1, 0):
+                far_copy(axis, False).wait_recv()
+                for p, _ in xs:
+                    start(share_copy(axis, p, True))
+        if step < 3:
+            drain(22)
+    for axis in (1, 0):
+        for p, _ in xs:
+            share_copy(axis, p, False).wait_recv()
     own_b = remote(all_b.at[z], sib_b, so.at[1], ro.at[1], sibling)
     start(own_b)
 
@@ -322,17 +361,11 @@
     atom_out[:, theirs] = sibs
     update += dot(dot(hot, ours).astype(BF16), w_tgt_ref[mine, :])
     update += dot(dot(hot, sibs).astype(BF16), w_tgt_ref[theirs, :])
+    drain(1)
     remote(pick_snd, pick_rcv, sp, rp, sibling).wait_recv()
     update += dot(pick_rcv[...], w_src_ref[theirs, :])
     edge_out[...] = (mid_ref[...].astype(F32) + silu(update)).astype(BF16)
-    for copy in waiting:
-        copy.wait_send()
-
-    def sent(i, carry):
-        copy_to(i)[1].wait_send()
-        return carry
-
-    lax.fori_loop(1, WIDE, sent, 0)
+    drain(0)
 
 
 def dma(*shape):
@@ -383,7 +416,8 @@
             pltpu.VMEM((512, 256), BF16),
             pltpu.VMEM((EDGES * BASIS, 256), BF16),
             pltpu.VMEM((EDGES, TILE), F32),
-            pltpu.VMEM((EDGES * TRIPLETS, 256), F32),
+            pltpu.VMEM((EDGES * TRIPLETS, TILE), F32),
+            pltpu.VMEM((EDGES * TRIPLETS, 512), BF16),
             pltpu.VMEM((EDGES, BASIS * TRIP), F32),
             dma(WIDE),
             dma(WIDE),
@@ -399,8 +433,8 @@
             pltpu.VMEM((6, TILE, TILE), I32),
             dma(NX), dma(NX), dma(NX), dma(NX), dma(NY), dma(NY),
             *semaphores(4),
-            dma(NX), dma(NX), dma(NZ), dma(NZ), dma(NY), dma(NY), dma(NX), dma(NX),
-            dma(64), dma(64), dma(2), dma(2),
+            dma(NX * NY), dma(NX * NY), dma(NX * NZ), dma(NX * NZ),
+            dma(64), dma(64), dma(2), dma(2), dma(2 * NX), dma(2 * NX), dma(2), dma(2),
             *semaphores(2),
         ],
         compiler_params=pltpu.CompilerParams(

time: 83.6 us -> 80.5 us (0.963)
  Pallas kernels: 79.6 us -> 77 us
    pallas_call x1, Pallas kernels: 79.6 us -> 77 us  [per_device(): pl.pallas_call(kernel, out_shape=(jax.ShapeDtypeStruct((EDGES, WIDTH), BF...]
where the time goes in v3:
time: 80.5 us; the launch traced here: 80.3 us
  Pallas kernels  77 us (96%)
  local copies, waits for them, and re-layouts  2.72 us (3%)
    pallas_call x1, Pallas kernels, per_device(): pl.pallas_call(kernel, out_shape=(jax.ShapeDtypeStruct((EDGES, WIDTH), BF...  77 us
    unnamed x4, local copies, waits for them, and re-layouts  2.72 us

profile of v3, /device:TPU:1, one launch (start us, length us, event | category | flops | bytes accessed | tf_op | source)
XLA Modules:
  0.0 80.3 jit_solution(8392205681913486390)
XLA Ops:
  0.6 77.0 %block.1 = (bf16[256,1024]{1,0:T(8,128)(2,1)}, bf16[512,512]{1,0:T(8,128)(2,1)}) custom-call(s32[1,256]{1,0:T(1,128)} %bitcast.10, s32[1,256]{1,0:T(1,128)} %bitcast.11, f32[1,512]{1,0:T(1,128)} %bitcast.9, bf16[256,1024]{1,0:T(8,128)(2,1)} %msg_hbm.1, s32[1,2048]{1,0:T(1,128)} %rows_hbm.1, bf16[64,1024]{1,0:T(8,128)(2,1)} %bitcast.6, ...), custom_call_target="tpu_custom_call" | custom-call | tf_op jit(solution)/shard_map/block/pallas_call | solution.py:391
  77.6 0.0 copy-start
  77.6 1.9 %copy.19 = bf16[256,1024]{1,0:T(8,128)(2,1)} copy(bf16[256,1024]{1,0:T(8,128)(2,1)} %get-tuple-element.4) | data formatting | bytes 1048576
  79.6 0.0 copy-done
  79.6 0.8 copy.20
Async XLA Ops:
  77.6 1.9 %copy-start = (bf16[512,512]{1,0:T(8,128)(2,1)S(1)}, bf16[512,512]{1,0:T(8,128)(2,1)}, u32[]{:S(2)}) copy-start(bf16[512,512]{1,0:T(8,128)(2,1)} %get-tuple-element.5) | copy-start | bytes 1572868

commit v4 on v3

--- a/solution.py
+++ b/solution.py
@@ -90,7 +90,7 @@
         pl.semaphore_signal(barrier, inc=1, device_id=(lax.rem(me + i, WIDE), row), device_id_type=MESH)
         return carry
 
-    lax.fori_loop(1, WIDE, greet, 0)
+    lax.fori_loop(1, WIDE, greet, 0, unroll=7)
     for px in range(NX):
         for p, _ in zs:
             pl.semaphore_signal(barrier, inc=1, device_id=at(px, y, c, p), device_id_type=MESH)
@@ -117,7 +117,7 @@
         copy_to(i)[1].start()
         return carry
 
-    lax.fori_loop(1, WIDE, send, 0)
+    lax.fori_loop(1, WIDE, send, 0, unroll=7)
     in_buf[me] = out_buf[me]
 
     for load in loads[3:5]:
@@ -171,7 +171,7 @@
         remote(out_buf.at[peer], in_buf.at[peer], send_sem.at[peer], recv_sem.at[peer], (peer, row)).wait_recv()
         return carry
 
-    lax.fori_loop(1, WIDE, arrived, 0)
+    lax.fori_loop(1, WIDE, arrived, 0, unroll=7)
 
     received = in_buf[...].reshape(WIDE * 16, TILE)
     table[...] = jnp.concatenate([received[:512], received[512:]], axis=1)

time: 80.5 us -> 80 us (level)
  no operation moved by 1% of the time
where the time goes in v4:
time: 80 us; the launch traced here: 79.8 us
  Pallas kernels  76.5 us (96%)
  local copies, waits for them, and re-layouts  2.72 us (3%)
    pallas_call x1, Pallas kernels, per_device(): pl.pallas_call(kernel, out_shape=(jax.ShapeDtypeStruct((EDGES, WIDTH), BF...  76.5 us
    unnamed x4, local copies, waits for them, and re-layouts  2.72 us

profile of v4, /device:TPU:1, one launch (start us, length us, event | category | flops | bytes accessed | tf_op | source)
XLA Modules:
  0.0 79.8 jit_solution(12379271513019516112)
XLA Ops:
  0.6 76.5 %block.1 = (bf16[256,1024]{1,0:T(8,128)(2,1)}, bf16[512,512]{1,0:T(8,128)(2,1)}) custom-call(s32[1,256]{1,0:T(1,128)} %bitcast.10, s32[1,256]{1,0:T(1,128)} %bitcast.11, f32[1,512]{1,0:T(1,128)} %bitcast.9, bf16[256,1024]{1,0:T(8,128)(2,1)} %msg_hbm.1, s32[1,2048]{1,0:T(1,128)} %rows_hbm.1, bf16[64,1024]{1,0:T(8,128)(2,1)} %bitcast.6, ...), custom_call_target="tpu_custom_call" | custom-call | tf_op jit(solution)/shard_map/block/pallas_call | solution.py:391
  77.1 0.0 copy-start
  77.1 1.9 %copy.19 = bf16[256,1024]{1,0:T(8,128)(2,1)} copy(bf16[256,1024]{1,0:T(8,128)(2,1)} %get-tuple-element.4) | data formatting | bytes 1048576
  79.0 0.0 copy-done
  79.0 0.8 copy.20
Async XLA Ops:
  77.1 1.9 %copy-start = (bf16[512,512]{1,0:T(8,128)(2,1)S(1)}, bf16[512,512]{1,0:T(8,128)(2,1)}, u32[]{:S(2)}) copy-start(bf16[512,512]{1,0:T(8,128)(2,1)} %get-tuple-element.5) | copy-start | bytes 1572868
